TPU v7x, 32 devices: a whole 2x2x4 slice. The times are simulated.
32 devices in a mesh: grp: 2 (over y), aux: 4 (over z), occ: 4 (over x, core).
Axes of the slice: x: 2, y: 2, z: 4, core: 2. Of those that a mesh axis runs over, the one named last changes fastest.
Arguments:
- b_factors: bfloat16 [16, 960, 512], P(('grp', 'occ'), 'aux'), parts along dimension 0, may hold values from -2.5 to 2.5
- tile_mask: int32 [16, 8], P('grp'), parts along dimension 0, may hold values 0 or 1
- batch_list: int32 [16], P('grp'), parts along dimension 0, may hold values from 0 to 499, as said below
- occ_energy: float32 [500], replicated, may hold values from -2 to -0.3
- vir_energy: float32 [512], P('aux'), may hold values from 0.2 to 4
Outputs:
- gamma: float32 [16, 960, 512], P(('grp', 'occ'), 'aux'), parts along dimension 0
There are 2 independent parts, one for each index of `grp`. A program takes and returns all parts, laid end to end along the dimension named above; an argument that names none is the same for every part. Nothing has to cross between parts.
Inputs may be any that keep to these rules, and one draw needn't show every extreme that they name: `batch_list`: entries are distinct; the first and the last occupied orbital of the molecule are always among them.
All inputs are finite; a program needn't handle non-finite values.
Results may differ from a plain program's by a relative error of at most 0.002.
Values may be sent and summed in bfloat16 or wider, within the bound.
A program may use at most 128 MiB of HBM per device.

v0:
```python
import jax
import jax.numpy as jnp
from jax import lax
from jax.sharding import PartitionSpec as P

VBLK = 128
TILE = 64


def pair_weights(coulomb, energy_mine, energy_other, energy_vir, mask_mine, mask_other):
    denominator = (
        energy_mine[:, None, None, None]
        + energy_other[None, None, :, None]
        - energy_vir[None, :, None, None]
        - energy_vir[None, None, None, :]
    )
    amplitude = coulomb * mask_mine[:, :, None, None] * mask_other[None, None, :, :] / denominator
    combined = 2.0 * amplitude - jnp.swapaxes(amplitude, 1, 3)
    return combined.astype(jnp.bfloat16)


def batch_energy(orbitals, occ_energy):
    hits = orbitals[:, None] == jnp.arange(occ_energy.shape[0], dtype=jnp.int32)[None, :]
    return jnp.sum(jnp.where(hits, occ_energy[None, :], jnp.float32(0.0)), axis=1)


def domain_mask(masks, domain_index):
    tiles_per = VBLK // TILE
    tiles = lax.dynamic_slice_in_dim(masks, domain_index * tiles_per, tiles_per, 1)
    return jnp.repeat(tiles.astype(jnp.float32), TILE, axis=1)


def density_terms(panel, partner, energy_mine, energy_other, vir_energy, mask_mine, mask_other):
    coulomb = jnp.einsum("iqa,jqb->iajb", panel, partner, preferred_element_type=jnp.float32)
    weights = pair_weights(coulomb, energy_mine, energy_other, vir_energy, mask_mine, mask_other)
    return jnp.einsum("iajb,jqb->iqa", weights, partner, preferred_element_type=jnp.float32)


def shards(b_factors, tile_mask, batch_list, occ_energy, vir_energy):
    own_count = b_factors.shape[0]
    domain_index = lax.axis_index("aux")
    own_first = lax.axis_index("occ") * own_count
    energy_all = batch_energy(batch_list, occ_energy)
    mask_all = domain_mask(tile_mask, domain_index)
    energy_mine = lax.dynamic_slice_in_dim(energy_all, own_first, own_count, 0)
    mask_mine = lax.dynamic_slice_in_dim(mask_all, own_first, own_count, 0)
    panel = lax.all_to_all(b_factors, "aux", split_axis=2, concat_axis=1, tiled=True)
    density = density_terms(
        panel,
        lax.all_gather(panel, "occ", axis=0, tiled=True),
        energy_mine,
        energy_all,
        vir_energy,
        mask_mine,
        mask_all,
    )
    return lax.all_to_all(density, "aux", split_axis=1, concat_axis=2, tiled=True)


def solution(mesh):
    in_specs = (P(("grp", "occ"), "aux", None), P("grp", None), P("grp"), P(), P("aux"))
    out_specs = P(("grp", "occ"), "aux", None)
    return jax.shard_map(shards, mesh=mesh, in_specs=in_specs, out_specs=out_specs, check_vma=False)
```

profile of v0, /device:TPU:0, one launch (start us, length us, event | category | flops | bytes accessed | tf_op | source)
XLA Modules:
  0.0 95.6 jit_solution(17785913533714303842)
XLA Ops:
  6.5 0.0 all-gather.2.cloned.1.call-start
  6.6 1.4 %copy.16 = bf16[2,240,512]{1,0,2:T(2,128)(2,1)S(1)} copy(bf16[2,240,512]{2,1,0:T(8,128)(2,1)} %param.5) | data formatting | bytes 983040 | tf_op args[0]
  7.9 20.6 %all_to_all.36 = bf16[2,240,512]{1,0,2:T(2,128)(2,1)S(1)} all-to-all(bf16[2,240,512]{1,0,2:T(2,128)(2,1)S(1)} %copy.16), channel_id=1, replica_groups=mesh['grp'=2,'aux'=4,'occ'=4] {'aux'}, dimensions={2} | all-to-all | bytes 983040 | tf_op jit(solution)/shard_map/all_to_all | solution.py:47
  28.6 1.1 %copy.17 = bf16[2,240,4,128]{3,1,2,0:T(8,128)(2,1)} copy(bf16[2,240,4,128]{1,0,3,2:T(2,128)(2,1)S(1)} %bitcast.39) | data formatting | bytes 983040 | tf_op jit(solution)/shard_map/all_to_all | solution.py:47
  29.6 0.0 all-gather.2.cloned.1.call-update
  29.7 0.0 copy-done.1
  29.7 0.1 dynamic-slice_convert_fusion
  29.7 0.1 broadcast_in_dim.14
  29.8 0.1 reshape.46
  29.9 0.0 copy-done.3
  29.9 0.0 copy-done.4
  29.9 0.2 select_reduce_fusion
  30.1 0.1 dynamic_slice.11
  30.2 0.1 broadcast_add_fusion
  30.3 0.1 broadcast_subtract_fusion
  30.3 0.1 broadcast_subtract_fusion.1
  30.4 20.4 %all-gather.2.cloned.1.call-done = bf16[8,960,128]{2,1,0:T(8,128)(2,1)} async-done(((bf16[2,960,128]{2,1,0:T(8,128)(2,1)}), bf16[8,960,128]{2,1,0:T(8,128)(2,1)}) %all-gather.2.cloned.1.call-update) | async-done | bytes 1966096 | tf_op jit(solution)/shard_map/all_gather | solution.py:50
  50.8 2.6 %fusion.4 = f32[2,128,8,128]{3,1,2,0:T(8,128)S(1)} fusion(bf16[2,960,128,1]{2,1,3,0:T(8,128)(2,1)} %bitcast.37, bf16[8,960,128]{2,1,0:T(8,128)(2,1)} %all-gather.2.cloned.1.call-done, f32[2,128]{1,0:T(2,128)S(1)} %constant_dynamic-slice_fusion), kind=kOutput, calls=%fused_computation.4 | convolution fusion | flops 503578624 | bytes 3507200 | tf_op jit(solution)/shard_map/iqa,jqb->iajb/dot_general | solution.py:34
  53.3 1.3 %copy.18 = f32[2,128,8,128]{1,3,2,0:T(8,128)} copy(f32[2,128,8,128]{3,1,2,0:T(8,128)S(1)} %fusion.4) | data formatting | bytes 2097152 | tf_op jit(solution)/shard_map/mul | solution.py:17
  54.7 2.2 %fusion.7 = f32[2,960,128]{2,1,0:T(8,128)S(1)} fusion(bf16[8,960,128]{2,1,0:T(8,128)(2,1)S(1)} %copy-done, f32[2,128,8,128]{3,1,2,0:T(8,128)S(1)} %fusion.4, f32[2,128,8,128]{1,3,2,0:T(8,128)} %copy.18, f32[128]{0:T(128)S(1)} %copy-done.2, f32[2,8,128]{2,1,0:T(8,128)S(1)} %broadcast_subtract_fusion, f32[128,8]{0,1:T(8,128)S(1)} %bitcast.40, ...), kind=kOutput, calls=%fused_computation.5 | convolution fusion | flops 505675776 | bytes 5071360 | tf_op jit(solution)/shard_map/iajb,jqb->iqa/dot_general | solution.py:36
  56.9 0.8 copy.20
  57.6 29.1 %all_to_all.37 = f32[2,960,128]{2,0,1:T(2,128)S(1)} all-to-all(f32[2,960,128]{2,0,1:T(2,128)S(1)} %copy.20), channel_id=1, replica_groups=mesh['grp'=2,'aux'=4,'occ'=4] {'aux'}, dimensions={1} | all-to-all | bytes 1966080 | tf_op jit(solution)/shard_map/all_to_all | solution.py:57
  86.8 0.6 copy.21
  87.4 1.3 %all_to_all.33 = f32[2,240,512]{2,1,0:T(8,128)} reshape(f32[2,240,4,128]{3,2,1,0:T(4,128)S(1)} %copy.21) | data formatting | bytes 1966080 | tf_op jit(solution)/shard_map/all_to_all | solution.py:57
  (8 shorter events, 0.0 us)
Async XLA Ops:
  6.5 23.1 %copy-start.1 = (s32[8,8]{1,0:T(8,128)S(1)}, s32[8,8]{1,0:T(8,128)}, u32[]{:S(2)}) copy-start(s32[8,8]{1,0:T(8,128)} %param.6) | copy-start | bytes 772
  6.5 23.4 %copy-start.3 = (f32[500]{0:T(512)S(1)}, f32[500]{0:T(512)}, u32[]{:S(2)}) copy-start(f32[500]{0:T(512)} %param.8) | copy-start | bytes 6004
  6.5 23.4 %copy-start.4 = (s32[8]{0:T(128)S(1)}, s32[8]{0:T(128)}, u32[]{:S(2)}) copy-start(s32[8]{0:T(128)} %param.7) | copy-start | bytes 100
  6.5 23.7 %copy-start.2 = (f32[128]{0:T(128)S(1)}, f32[128]{0:T(128)}, u32[]{:S(2)}) copy-start(f32[128]{0:T(128)} %param.9) | copy-start | bytes 1540
  6.5 44.2 %all-gather.2.cloned.1.call-start = ((), (), s32[]{:S(2)}) async-start(), calls=%async_computation.2 | async-start | bytes 2457600 | tf_op jit(solution)/shard_map/all_gather | solution.py:50
  50.8 3.9 %copy-start = (bf16[8,960,128]{2,1,0:T(8,128)(2,1)S(1)}, bf16[8,960,128]{2,1,0:T(8,128)(2,1)}, u32[]{:S(2)}) copy-start(bf16[8,960,128]{2,1,0:T(8,128)(2,1)} %all-gather.2.cloned.1.call-done) | copy-start | bytes 5898244
Sparse Core Ops, SparseCore 0:
  29.8 20.9 all-gather.1
where the time goes:
time: 95.8 us; the launch traced here: 95.6 us
  blocking collectives  49.7 us (52%)
  waiting for transfers between devices  20.4 us (21%)
  between operations  13.5 us (14%)
  local copies, waits for them, and re-layouts  6.75 us (7%)
  matrix products  4.75 us (5%)
    all_to_all x1, blocking collectives, shards(): lax.all_to_all(density, 'aux', split_axis=1, concat_axis=2, tiled=True)  29.1 us
    all_to_all x1, blocking collectives, shards(): lax.all_to_all(b_factors, 'aux', split_axis=2, concat_axis=1, tiled=True)  20.6 us
    all_gather x1, waiting for transfers between devices, shards(): lax.all_gather(panel, 'occ', axis=0, tiled=True)  20.4 us
    dot_general x1, matrix products, density_terms(): jnp.einsum('iqa,jqb->iajb', panel, partner, preferred_element_type=jnp.fl...  2.56 us
    dot_general x1, matrix products, density_terms(): jnp.einsum('iajb,jqb->iqa', weights, partner, preferred_element_type=jnp....  2.19 us
    all_to_all x2, local copies, waits for them, and re-layouts, shards(): lax.all_to_all(density, 'aux', split_axis=1, concat_axis=2, tiled=True)  1.97 us
  transfers between devices with their start and end apart: 1, of which 1 were waited for; matrix products, arithmetic and copies ran while one was open for 1% of the time, Pallas kernels for 0%

commit v1 on v0

v1 whole, which is shorter than its diff:
```python
import functools

import jax
import jax.numpy as jnp
from jax import lax
from jax.experimental import pallas as pl
from jax.experimental.pallas import tpu as pltpu
from jax.sharding import PartitionSpec as P

VBLK = 128
TILE = 64
OCC = 4


def flip(index, bits):
    bit = 1
    while bit <= bits:
        if bits & bit:
            index = index + bit - 2 * bit * (lax.div(index, bit) % 2)
        bit *= 2
    return index


def send_order(n):
    return [k for k in range(1, n) if 2 * k >= n] + [k for k in range(1, n) if 2 * k < n]


def kernel(
    n,
    b_ref,
    tile_ref,
    batch_ref,
    occ_ref,
    vir_ref,
    out_ref,
    gath,
    coul,
    w_dir,
    w_exc,
    amp,
    outgoing,
    incoming,
    own_sem,
    z_send,
    z_recv,
    f_send,
    f_recv,
    r_send,
    r_recv,
):
    own = b_ref.shape[0]
    width = own * VBLK
    z = lax.axis_index("aux")
    o = lax.axis_index("occ")
    zs = [flip(z, k) for k in range(n)]
    os = [flip(o, r) for r in range(OCC)]

    def columns(k):
        return pl.ds(pl.multiple_of(zs[k] * VBLK, VBLK), VBLK)

    def remote(src, dst, send_sem, recv_sem, **where):
        return pltpu.make_async_remote_copy(
            src_ref=src,
            dst_ref=dst,
            send_sem=send_sem,
            recv_sem=recv_sem,
            device_id=where,
            device_id_type=pl.DeviceIdType.MESH,
        )

    own_copy = pltpu.make_async_copy(b_ref.at[:, :, columns(0)], gath.at[0, 0], own_sem)
    own_copy.start()

    barrier = pltpu.get_barrier_semaphore()
    for k in range(1, n):
        pl.semaphore_signal(barrier, inc=1, device_id={"aux": zs[k]}, device_id_type=pl.DeviceIdType.MESH)
    for r in (1, 2):
        pl.semaphore_signal(barrier, inc=1, device_id={"occ": os[r]}, device_id_type=pl.DeviceIdType.MESH)
    pl.semaphore_wait(barrier, n + 1)

    far_first = send_order(n)
    z_copies = {}
    for k in far_first:
        z_copies[k] = remote(b_ref.at[:, :, columns(k)], gath.at[0, k], z_send.at[k], z_recv.at[k], aux=zs[k])
        z_copies[k].start()
    near = [remote(gath.at[0, k], gath.at[1, k], f_send.at[0, k], f_recv.at[0, k], occ=os[1]) for k in range(n)]
    cross = [remote(gath.at[0, k], gath.at[2, k], f_send.at[1, k], f_recv.at[1, k], occ=os[2]) for k in range(n)]
    onward = [remote(gath.at[2, k], gath.at[3, k], f_send.at[2, k], f_recv.at[2, k], occ=os[1]) for k in range(n)]

    own_copy.wait()
    cross[0].start()
    near[0].start()

    orbitals = [[os[r] * own + i for i in range(own)] for r in range(OCC)]
    energy = [[occ_ref[batch_ref[j]] for j in row] for row in orbitals]
    tiles = VBLK // TILE
    mask = [
        [[tile_ref[j, z * tiles + t].astype(jnp.float32) for t in range(tiles)] for j in row] for row in orbitals
    ]
    lane_tile = lax.broadcasted_iota(jnp.int32, (1, VBLK), 1) // TILE

    def row_mask(values):
        row = jnp.full((1, VBLK), values[0], jnp.float32)
        for t in range(1, tiles):
            row = jnp.where(lane_tile == t, values[t], row)
        return row

    rows = [[row_mask(m) for m in entry] for entry in mask]
    vir = jnp.broadcast_to(vir_ref[...], (VBLK, VBLK))
    vir_sum = vir + vir.T
    for r in range(OCC):
        for jj in range(own):
            for i in range(own):
                inverse = 1.0 / ((energy[0][i] + energy[r][jj]) - vir_sum)
                for t in range(tiles):
                    part = inverse[t * TILE : (t + 1) * TILE]
                    at = pl.ds((r * own + jj) * VBLK + t * TILE, TILE)
                    to = pl.ds(i * VBLK, VBLK)
                    w_dir[at, to] = part * (rows[0][i] * (2.0 * mask[r][jj][t]))
                    w_exc[at, to] = part * (rows[r][jj] * mask[0][i][t])

    def wide(r, k):
        return jnp.concatenate([gath[r, k, i] for i in range(own)], axis=1)

    def add_chunk(k, first):
        mine = wide(0, k)
        for r in range(OCC):
            term = lax.dot_general(
                mine, wide(r, k), (((0,), (0,)), ((), ())), preferred_element_type=jnp.float32
            )
            at = pl.ds(r * width, width)
            if first:
                coul[:, at] = term
            else:
                coul[:, at] += term

    order = [0] + far_first[::-1]
    for step in range(n + 2):
        if 0 < step < n:
            k = order[step]
            z_copies[k].wait_recv()
            cross[k].start()
            near[k].start()
        if 1 <= step < n + 1:
            k = order[step - 1]
            cross[k].wait_recv()
            onward[k].start()
        if step >= 2:
            k = order[step - 2]
            near[k].wait_recv()
            onward[k].wait_recv()
            add_chunk(k, step == 2)

    for r in range(OCC):
        for jj in range(own):
            for i in range(own):
                block = coul[pl.ds(i * VBLK, VBLK), pl.ds((r * own + jj) * VBLK, VBLK)]
                at = pl.ds((r * own + jj) * VBLK, VBLK)
                to = pl.ds(i * VBLK, VBLK)
                amp[at, to] = (block.T * w_dir[at, to] - block * w_exc[at, to]).astype(jnp.bfloat16)

    def density(k):
        total = jnp.dot(wide(0, k), amp[pl.ds(0, width)], preferred_element_type=jnp.float32)
        for r in range(1, OCC):
            total += jnp.dot(wide(r, k), amp[pl.ds(r * width, width)], preferred_element_type=jnp.float32)
        return total

    back = {}
    for k in far_first:
        total = density(k)
        for i in range(own):
            outgoing[k, i] = total[:, i * VBLK : (i + 1) * VBLK].astype(jnp.bfloat16)
        back[k] = remote(outgoing.at[k], incoming.at[k], r_send.at[k], r_recv.at[k], aux=zs[k])
        back[k].start()
    total = density(0)
    for i in range(own):
        out_ref[i, :, columns(0)] = total[:, i * VBLK : (i + 1) * VBLK]

    for k in far_first[::-1]:
        back[k].wait_recv()
        for i in range(own):
            out_ref[i, :, columns(k)] = incoming[k, i].astype(jnp.float32)

    for k in range(n):
        near[k].wait_send()
        cross[k].wait_send()
        onward[k].wait_send()
        if k:
            z_copies[k].wait_send()
            back[k].wait_send()


def shards(n, b_factors, tile_mask, batch_list, occ_energy, vir_energy):
    own, depth, columns = b_factors.shape
    width = own * VBLK
    dma = pltpu.SemaphoreType.DMA
    chunk = (own, depth, VBLK)
    chunk_bytes = own * depth * VBLK * 2
    pair_bytes = OCC * width * width * 4
    need = (OCC + 2) * n * chunk_bytes + 4 * pair_bytes + 2 * n * chunk_bytes
    vmem = pl.BlockSpec(memory_space=pltpu.VMEM)
    smem = pl.BlockSpec(memory_space=pltpu.SMEM)
    return pl.pallas_call(
        functools.partial(kernel, n),
        out_shape=jax.ShapeDtypeStruct(b_factors.shape, jnp.float32),
        in_specs=[pl.BlockSpec(memory_space=pl.ANY), smem, smem, smem, vmem],
        out_specs=vmem,
        scratch_shapes=[
            pltpu.VMEM((OCC, n) + chunk, jnp.bfloat16),
            pltpu.VMEM((width, OCC * width), jnp.float32),
            pltpu.VMEM((OCC * width, width), jnp.float32),
            pltpu.VMEM((OCC * width, width), jnp.float32),
            pltpu.VMEM((OCC * width, width), jnp.bfloat16),
            pltpu.VMEM((n,) + chunk, jnp.bfloat16),
            pltpu.VMEM((n,) + chunk, jnp.bfloat16),
            dma,
            dma((n,)),
            dma((n,)),
            dma((3, n)),
            dma((3, n)),
            dma((n,)),
            dma((n,)),
        ],
        compiler_params=pltpu.CompilerParams(
            collective_id=0, has_side_effects=True, vmem_limit_bytes=need + (12 << 20)
        ),
    )(b_factors, tile_mask, batch_list, occ_energy, vir_energy[None, :])


def solution(mesh):
    in_specs = (P(("grp", "occ"), "aux", None), P("grp", None), P("grp"), P(), P("aux"))
    out_specs = P(("grp", "occ"), "aux", None)
    return jax.shard_map(
        functools.partial(shards, mesh.shape["aux"]), mesh=mesh, in_specs=in_specs, out_specs=out_specs, check_vma=False
    )
```

time: 95.8 us -> 40.2 us (0.42)
  blocking collectives: 49.7 us -> 0 us
  Pallas kernels: 0 us -> 35.9 us
  waiting for transfers between devices: 20.4 us -> 0 us
  between operations: 13.5 us -> 0.01 us
  matrix products: 4.75 us -> 0 us
  local copies, waits for them, and re-layouts: 6.75 us -> 4.01 us
    all_to_all x2 -> x0, blocking collectives: 49.7 us -> none  [the longest x1 29.1 us: shards(): lax.all_to_all(density, 'aux', split_axis=1, concat_axis=2, tiled=True)]
    pallas_call x0 -> x1, Pallas kernels: none -> 35.9 us  [shards(): pl.pallas_call(functools.partial(kernel, n), out_shape=jax.ShapeDtypeStru...]
    all_gather x1 -> x0, waiting for transfers between devices: 20.4 us -> none  [shards(): lax.all_gather(panel, 'occ', axis=0, tiled=True)]
    dot_general x2 -> x0, matrix products: 4.75 us -> none  [the longest x1 2.56 us: density_terms(): jnp.einsum('iqa,jqb->iajb', panel, partner, preferred_element_type=jnp.fl...]
    all_to_all x3 -> x0, local copies, waits for them, and re-layouts: 3.04 us -> none  [the longest x2 1.97 us: shards(): lax.all_to_all(density, 'aux', split_axis=1, concat_axis=2, tiled=True)]
    unnamed x11, local copies, waits for them, and re-layouts: 1.38 us -> 4.01 us
    mul x1 -> x0, local copies, waits for them, and re-layouts: 1.33 us -> none  [pair_weights(): coulomb * mask_mine[:, :, None, None] * mask_other[None, None, :, :]]
  transfers between devices with their start and end apart: 1 -> 0, of which waited for: 1 -> 0; matrix products, arithmetic and copies ran while one was open for 1% -> 0% of each run, Pallas kernels for 0% -> 0%
where the time goes in v1:
time: 40.2 us; the launch traced here: 40 us
  Pallas kernels  35.9 us (89%)
  local copies, waits for them, and re-layouts  4.01 us (10%)
    pallas_call x1, Pallas kernels, shards(): pl.pallas_call(functools.partial(kernel, n), out_shape=jax.ShapeDtypeStru...  35.9 us
    unnamed x11, local copies, waits for them, and re-layouts  4.01 us

profile of v1, /device:TPU:0, one launch (start us, length us, event | category | flops | bytes accessed | tf_op | source)
XLA Modules:
  0.0 40.0 jit_solution(48883508086640085)
XLA Ops:
  0.0 0.0 copy-start.4
  0.0 0.0 copy-start.3
  0.0 0.7 %copy-done.4 = f32[128]{0:T(128)S(1)} copy-done((f32[128]{0:T(128)S(1)}, f32[128]{0:T(128)}, u32[]{:S(2)}) %copy-start.4) | copy-done | bytes 536
  0.7 0.0 copy-done.3
  0.7 0.0 copy-start
  0.7 1.0 %copy-done = bf16[2,240,512]{2,1,0:T(8,128)(2,1)S(1)} copy-done((bf16[2,240,512]{2,1,0:T(8,128)(2,1)S(1)}, bf16[2,240,512]{2,1,0:T(8,128)(2,1)}, u32[]{:S(2)}) %copy-start) | copy-done | bytes 491544
  1.7 0.0 copy-start.1
  1.7 0.7 %copy-done.1 = s32[8,8]{1,0:T(8,128)S(1)} copy-done((s32[8,8]{1,0:T(8,128)S(1)}, s32[8,8]{1,0:T(8,128)}, u32[]{:S(2)}) %copy-start.1) | copy-done | bytes 280
  2.4 0.0 copy-start.2
  2.4 0.7 %copy-done.2 = f32[500]{0:T(512)S(1)} copy-done((f32[500]{0:T(512)S(1)}, f32[500]{0:T(512)}, u32[]{:S(2)}) %copy-start.2) | copy-done | bytes 2024
  3.1 35.9 %shard_map.55 = f32[2,240,512]{2,1,0:T(8,128)S(1)} custom-call(bf16[2,240,512]{2,1,0:T(8,128)(2,1)S(1)} %copy-done, s32[8,8]{1,0:T(8,128)S(1)} %copy-done.1, s32[8]{0:T(128)S(1)} %copy-done.3, f32[500]{0:T(512)S(1)} %copy-done.2, f32[1,128]{1,0:T(1,128)S(1)} %bitcast.1), custom_call_target="tpu_custom_call" | custom-call | tf_op jit(solution)/shard_map/pallas_call | solution.py:203
  39.0 0.9 %copy.7 = f32[2,240,512]{2,1,0:T(8,128)} copy(f32[2,240,512]{2,1,0:T(8,128)S(1)} %shard_map.55) | data formatting | bytes 1966080
Async XLA Ops:
  0.0 0.7 %copy-start.4 = (f32[128]{0:T(128)S(1)}, f32[128]{0:T(128)}, u32[]{:S(2)}) copy-start(f32[128]{0:T(128)} %param.9) | copy-start | bytes 1540
  0.0 0.7 %copy-start.3 = (s32[8]{0:T(128)S(1)}, s32[8]{0:T(128)}, u32[]{:S(2)}) copy-start(s32[8]{0:T(128)} %batch_ref.1) | copy-start | bytes 100
  0.7 1.0 %copy-start = (bf16[2,240,512]{2,1,0:T(8,128)(2,1)S(1)}, bf16[2,240,512]{2,1,0:T(8,128)(2,1)}, u32[]{:S(2)}) copy-start(bf16[2,240,512]{2,1,0:T(8,128)(2,1)} %b_ref.1) | copy-start | bytes 1474564
  1.7 0.7 %copy-start.1 = (s32[8,8]{1,0:T(8,128)S(1)}, s32[8,8]{1,0:T(8,128)}, u32[]{:S(2)}) copy-start(s32[8,8]{1,0:T(8,128)} %tile_ref.1) | copy-start | bytes 772
  2.4 0.7 %copy-start.2 = (f32[500]{0:T(512)S(1)}, f32[500]{0:T(512)}, u32[]{:S(2)}) copy-start(f32[500]{0:T(512)} %occ_ref.1) | copy-start | bytes 6004

commit v2 on v1

--- a/solution.py
+++ b/solution.py
@@ -28,11 +28,15 @@
 def kernel(
     n,
     b_ref,
+    tile_hbm,
+    batch_hbm,
+    occ_hbm,
+    vir_hbm,
+    out_ref,
     tile_ref,
     batch_ref,
     occ_ref,
     vir_ref,
-    out_ref,
     gath,
     coul,
     w_dir,
@@ -41,12 +45,15 @@
     outgoing,
     incoming,
     own_sem,
+    small_sem,
     z_send,
     z_recv,
     f_send,
     f_recv,
     r_send,
     r_recv,
+    result,
+    store_sem,
 ):
     own = b_ref.shape[0]
     width = own * VBLK
@@ -69,7 +76,15 @@
         )
 
     own_copy = pltpu.make_async_copy(b_ref.at[:, :, columns(0)], gath.at[0, 0], own_sem)
+    small = [
+        pltpu.make_async_copy(src, dst, small_sem.at[j])
+        for j, (src, dst) in enumerate(
+            ((tile_hbm, tile_ref), (batch_hbm, batch_ref), (occ_hbm, occ_ref), (vir_hbm, vir_ref))
+        )
+    ]
     own_copy.start()
+    for copy in small:
+        copy.start()
 
     barrier = pltpu.get_barrier_semaphore()
     for k in range(1, n):
@@ -79,17 +94,34 @@
     pl.semaphore_wait(barrier, n + 1)
 
     far_first = send_order(n)
+    order = [0] + far_first[::-1]
+    pieces = [(k, i) for k in order for i in range(own)]
     z_copies = {}
-    for k in far_first:
-        z_copies[k] = remote(b_ref.at[:, :, columns(k)], gath.at[0, k], z_send.at[k], z_recv.at[k], aux=zs[k])
-        z_copies[k].start()
-    near = [remote(gath.at[0, k], gath.at[1, k], f_send.at[0, k], f_recv.at[0, k], occ=os[1]) for k in range(n)]
-    cross = [remote(gath.at[0, k], gath.at[2, k], f_send.at[1, k], f_recv.at[1, k], occ=os[2]) for k in range(n)]
-    onward = [remote(gath.at[2, k], gath.at[3, k], f_send.at[2, k], f_recv.at[2, k], occ=os[1]) for k in range(n)]
+    for k, i in pieces[own:]:
+        z_copies[k, i] = remote(
+            b_ref.at[i, :, columns(k)], gath.at[0, k, i], z_send.at[k, i], z_recv.at[k, i], aux=zs[k]
+        )
+        z_copies[k, i].start()
+
+    def passing(kind, source, target, partner):
+        return {
+            (k, i): remote(
+                gath.at[source, k, i], gath.at[target, k, i], f_send.at[kind, k, i], f_recv.at[kind, k, i], occ=os[partner]
+            )
+            for k, i in pieces
+        }
+
+    near = passing(0, 0, 1, 1)
+    cross = passing(1, 0, 2, 2)
+    onward = passing(2, 2, 3, 1)
 
     own_copy.wait()
-    cross[0].start()
-    near[0].start()
+    for i in range(own):
+        cross[0, i].start()
+    for i in range(own):
+        near[0, i].start()
+    for copy in small:
+        copy.wait()
 
     orbitals = [[os[r] * own + i for i in range(own)] for r in range(OCC)]
     energy = [[occ_ref[batch_ref[j]] for j in row] for row in orbitals]
@@ -134,22 +166,23 @@
             else:
                 coul[:, at] += term
 
-    order = [0] + far_first[::-1]
-    for step in range(n + 2):
-        if 0 < step < n:
-            k = order[step]
-            z_copies[k].wait_recv()
-            cross[k].start()
-            near[k].start()
-        if 1 <= step < n + 1:
-            k = order[step - 1]
-            cross[k].wait_recv()
-            onward[k].start()
-        if step >= 2:
-            k = order[step - 2]
-            near[k].wait_recv()
-            onward[k].wait_recv()
-            add_chunk(k, step == 2)
+    lag = own
+    for step in range(len(pieces) + 2 * lag):
+        if own <= step < len(pieces):
+            piece = pieces[step]
+            z_copies[piece].wait_recv()
+            cross[piece].start()
+            near[piece].start()
+        if lag <= step < len(pieces) + lag:
+            piece = pieces[step - lag]
+            cross[piece].wait_recv()
+            onward[piece].start()
+        if step >= 2 * lag:
+            piece = pieces[step - 2 * lag]
+            near[piece].wait_recv()
+            onward[piece].wait_recv()
+            if piece[1] == own - 1:
+                add_chunk(piece[0], piece[0] == 0)
 
     for r in range(OCC):
         for jj in range(own):
@@ -165,6 +198,9 @@
             total += jnp.dot(wide(r, k), amp[pl.ds(r * width, width)], preferred_element_type=jnp.float32)
         return total
 
+    stores = [
+        pltpu.make_async_copy(result.at[k], out_ref.at[:, :, columns(k)], store_sem.at[k]) for k in range(n)
+    ]
     back = {}
     for k in far_first:
         total = density(k)
@@ -174,20 +210,25 @@
         back[k].start()
     total = density(0)
     for i in range(own):
-        out_ref[i, :, columns(0)] = total[:, i * VBLK : (i + 1) * VBLK]
+        result[0, i] = total[:, i * VBLK : (i + 1) * VBLK]
+    stores[0].start()
 
     for k in far_first[::-1]:
         back[k].wait_recv()
         for i in range(own):
-            out_ref[i, :, columns(k)] = incoming[k, i].astype(jnp.float32)
-
-    for k in range(n):
-        near[k].wait_send()
-        cross[k].wait_send()
-        onward[k].wait_send()
-        if k:
-            z_copies[k].wait_send()
-            back[k].wait_send()
+            result[k, i] = incoming[k, i].astype(jnp.float32)
+        stores[k].start()
+
+    for piece in pieces:
+        near[piece].wait_send()
+        cross[piece].wait_send()
+        onward[piece].wait_send()
+        if piece[0]:
+            z_copies[piece].wait_send()
+    for k in far_first:
+        back[k].wait_send()
+    for copy in stores:
+        copy.wait()
 
 
 def shards(n, b_factors, tile_mask, batch_list, occ_energy, vir_energy):
@@ -198,14 +239,17 @@
     chunk_bytes = own * depth * VBLK * 2
     pair_bytes = OCC * width * width * 4
     need = (OCC + 2) * n * chunk_bytes + 4 * pair_bytes + 2 * n * chunk_bytes
-    vmem = pl.BlockSpec(memory_space=pltpu.VMEM)
-    smem = pl.BlockSpec(memory_space=pltpu.SMEM)
+    hbm = pl.BlockSpec(memory_space=pltpu.HBM)
     return pl.pallas_call(
         functools.partial(kernel, n),
         out_shape=jax.ShapeDtypeStruct(b_factors.shape, jnp.float32),
-        in_specs=[pl.BlockSpec(memory_space=pl.ANY), smem, smem, smem, vmem],
-        out_specs=vmem,
+        in_specs=[hbm] * 5,
+        out_specs=hbm,
         scratch_shapes=[
+            pltpu.SMEM(tile_mask.shape, jnp.int32),
+            pltpu.SMEM(batch_list.shape, jnp.int32),
+            pltpu.SMEM(occ_energy.shape, jnp.float32),
+            pltpu.VMEM((1, VBLK), jnp.float32),
             pltpu.VMEM((OCC, n) + chunk, jnp.bfloat16),
             pltpu.VMEM((width, OCC * width), jnp.float32),
             pltpu.VMEM((OCC * width, width), jnp.float32),
@@ -214,15 +258,18 @@
             pltpu.VMEM((n,) + chunk, jnp.bfloat16),
             pltpu.VMEM((n,) + chunk, jnp.bfloat16),
             dma,
+            dma((4,)),
+            dma((n, own)),
+            dma((n, own)),
+            dma((3, n, own)),
+            dma((3, n, own)),
             dma((n,)),
             dma((n,)),
-            dma((3, n)),
-            dma((3, n)),
-            dma((n,)),
+            pltpu.VMEM((n,) + chunk, jnp.float32),
             dma((n,)),
         ],
         compiler_params=pltpu.CompilerParams(
-            collective_id=0, has_side_effects=True, vmem_limit_bytes=need + (12 << 20)
+            collective_id=0, has_side_effects=True, vmem_limit_bytes=58000 << 10
         ),
     )(b_factors, tile_mask, batch_list, occ_energy, vir_energy[None, :])
 

time: 40.2 us -> 36.4 us (0.905); the launches traced: 40 us -> 35.6 us
  Pallas kernels: 35.9 us -> 33.4 us
  local copies, waits for them, and re-layouts: 4.01 us -> 2.21 us
    pallas_call x1, Pallas kernels: 35.9 us -> 33.4 us  [shards(): pl.pallas_call(functools.partial(kernel, n), out_shape=jax.ShapeDtypeStru...]
    unnamed x11 -> x1, local copies, waits for them, and re-layouts: 4.01 us -> 2.21 us
where the time goes in v2:
time: 36.4 us; the launch traced here: 35.6 us
  Pallas kernels  33.4 us (92%)
  local copies, waits for them, and re-layouts  2.21 us (6%)
    pallas_call x1, Pallas kernels, shards(): pl.pallas_call(functools.partial(kernel, n), out_shape=jax.ShapeDtypeStru...  33.4 us
    unnamed x1, local copies, waits for them, and re-layouts  2.21 us

profile of v2, /device:TPU:0, one launch (start us, length us, event | category | flops | bytes accessed | tf_op | source)
XLA Modules:
  0.0 35.6 jit_solution(13569056128832593416)
XLA Ops:
  0.0 33.4 %shard_map.55 = f32[2,240,512]{2,1,0:T(8,128)} custom-call(bf16[2,240,512]{2,1,0:T(8,128)(2,1)} %b_ref.1, s32[8,8]{1,0:T(8,128)} %tile_hbm.1, s32[8]{0:T(128)} %batch_hbm.1, f32[500]{0:T(512)} %occ_hbm.1, f32[1,128]{1,0:T(1,128)} %bitcast.1), custom_call_target="tpu_custom_call" | custom-call | tf_op jit(solution)/shard_map/pallas_call | solution.py:243
  33.4 2.2 %copy.7 = f32[2,240,512]{2,1,0:T(8,128)} copy(f32[2,240,512]{2,1,0:T(8,128)} %shard_map.55) | data formatting | bytes 1966080

commit v3 on v2

--- a/solution.py
+++ b/solution.py
@@ -43,7 +43,6 @@
     w_exc,
     amp,
     outgoing,
-    incoming,
     own_sem,
     small_sem,
     z_send,
@@ -52,7 +51,6 @@
     f_recv,
     r_send,
     r_recv,
-    result,
     store_sem,
 ):
     own = b_ref.shape[0]
@@ -74,6 +72,12 @@
             device_id=where,
             device_id_type=pl.DeviceIdType.MESH,
         )
+
+    barrier = pltpu.get_barrier_semaphore()
+    for k in range(1, n):
+        pl.semaphore_signal(barrier, inc=1, device_id={"aux": zs[k]}, device_id_type=pl.DeviceIdType.MESH)
+    for r in (1, 2):
+        pl.semaphore_signal(barrier, inc=1, device_id={"occ": os[r]}, device_id_type=pl.DeviceIdType.MESH)
 
     own_copy = pltpu.make_async_copy(b_ref.at[:, :, columns(0)], gath.at[0, 0], own_sem)
     small = [
@@ -85,12 +89,6 @@
     own_copy.start()
     for copy in small:
         copy.start()
-
-    barrier = pltpu.get_barrier_semaphore()
-    for k in range(1, n):
-        pl.semaphore_signal(barrier, inc=1, device_id={"aux": zs[k]}, device_id_type=pl.DeviceIdType.MESH)
-    for r in (1, 2):
-        pl.semaphore_signal(barrier, inc=1, device_id={"occ": os[r]}, device_id_type=pl.DeviceIdType.MESH)
     pl.semaphore_wait(barrier, n + 1)
 
     far_first = send_order(n)
@@ -198,26 +196,21 @@
             total += jnp.dot(wide(r, k), amp[pl.ds(r * width, width)], preferred_element_type=jnp.float32)
         return total
 
-    stores = [
-        pltpu.make_async_copy(result.at[k], out_ref.at[:, :, columns(k)], store_sem.at[k]) for k in range(n)
-    ]
     back = {}
     for k in far_first:
         total = density(k)
         for i in range(own):
             outgoing[k, i] = total[:, i * VBLK : (i + 1) * VBLK].astype(jnp.bfloat16)
-        back[k] = remote(outgoing.at[k], incoming.at[k], r_send.at[k], r_recv.at[k], aux=zs[k])
+        back[k] = remote(outgoing.at[k], out_ref.at[z], r_send.at[k], r_recv.at[k], aux=zs[k])
         back[k].start()
     total = density(0)
     for i in range(own):
-        result[0, i] = total[:, i * VBLK : (i + 1) * VBLK]
-    stores[0].start()
+        outgoing[0, i] = total[:, i * VBLK : (i + 1) * VBLK].astype(jnp.bfloat16)
+    store = pltpu.make_async_copy(outgoing.at[0], out_ref.at[z], store_sem)
+    store.start()
 
     for k in far_first[::-1]:
         back[k].wait_recv()
-        for i in range(own):
-            result[k, i] = incoming[k, i].astype(jnp.float32)
-        stores[k].start()
 
     for piece in pieces:
         near[piece].wait_send()
@@ -227,8 +220,7 @@
             z_copies[piece].wait_send()
     for k in far_first:
         back[k].wait_send()
-    for copy in stores:
-        copy.wait()
+    store.wait()
 
 
 def shards(n, b_factors, tile_mask, batch_list, occ_energy, vir_energy):
@@ -240,9 +232,9 @@
     pair_bytes = OCC * width * width * 4
     need = (OCC + 2) * n * chunk_bytes + 4 * pair_bytes + 2 * n * chunk_bytes
     hbm = pl.BlockSpec(memory_space=pltpu.HBM)
-    return pl.pallas_call(
+    slots = pl.pallas_call(
         functools.partial(kernel, n),
-        out_shape=jax.ShapeDtypeStruct(b_factors.shape, jnp.float32),
+        out_shape=jax.ShapeDtypeStruct((n,) + chunk, jnp.bfloat16),
         in_specs=[hbm] * 5,
         out_specs=hbm,
         scratch_shapes=[
@@ -256,7 +248,6 @@
             pltpu.VMEM((OCC * width, width), jnp.float32),
             pltpu.VMEM((OCC * width, width), jnp.bfloat16),
             pltpu.VMEM((n,) + chunk, jnp.bfloat16),
-            pltpu.VMEM((n,) + chunk, jnp.bfloat16),
             dma,
             dma((4,)),
             dma((n, own)),
@@ -265,13 +256,13 @@
             dma((3, n, own)),
             dma((n,)),
             dma((n,)),
-            pltpu.VMEM((n,) + chunk, jnp.float32),
-            dma((n,)),
+            dma,
         ],
         compiler_params=pltpu.CompilerParams(
             collective_id=0, has_side_effects=True, vmem_limit_bytes=58000 << 10
         ),
     )(b_factors, tile_mask, batch_list, occ_energy, vir_energy[None, :])
+    return jnp.concatenate([slots[k].astype(jnp.float32) for k in range(n)], axis=2)
 
 
 def solution(mesh):

time: 36.4 us -> 35.6 us (0.978)
  local copies, waits for them, and re-layouts: 2.21 us -> 1.11 us
  other arithmetic: 0 us -> 1.02 us
  Pallas kernels: 33.4 us -> 32.8 us
    unnamed x1 -> x0, local copies, waits for them, and re-layouts: 2.21 us -> none
    convert_element_type x0 -> x1, local copies, waits for them, and re-layouts: none -> 1.11 us  [shards(): slots[k].astype(jnp.float32)]
    concatenate x0 -> x1, other arithmetic: none -> 1.02 us  [shards(): jnp.concatenate([slots[k].astype(jnp.float32) for k in range(n)], axis=2)]
    pallas_call x1, Pallas kernels: 33.4 us -> 32.8 us  [shards(): pl.pallas_call(functools.partial(kernel, n), out_shape=jax.ShapeDtypeStru...]
where the time goes in v3:
time: 35.6 us; the launch traced here: 34.9 us
  Pallas kernels  32.8 us (92%)
  local copies, waits for them, and re-layouts  1.11 us (3%)
  other arithmetic  1.02 us (3%)
    pallas_call x1, Pallas kernels, shards(): pl.pallas_call(functools.partial(kernel, n), out_shape=jax.ShapeDtypeStru...  32.8 us
    convert_element_type x1, local copies, waits for them, and re-layouts, shards(): slots[k].astype(jnp.float32)  1.11 us
    concatenate x1, other arithmetic, shards(): jnp.concatenate([slots[k].astype(jnp.float32) for k in range(n)], axis=2)  1.02 us

profile of v3, /device:TPU:0, one launch (start us, length us, event | category | flops | bytes accessed | tf_op | source)
XLA Modules:
  0.0 34.9 jit_solution(3932438147183651932)
XLA Ops:
  0.0 32.8 %shard_map.55 = bf16[4,2,240,128]{3,2,1,0:T(8,128)(2,1)} custom-call(bf16[2,240,512]{2,1,0:T(8,128)(2,1)} %b_ref.1, s32[8,8]{1,0:T(8,128)} %tile_hbm.1, s32[8]{0:T(128)} %batch_hbm.1, f32[500]{0:T(512)} %occ_hbm.1, f32[1,128]{1,0:T(1,128)} %bitcast.9), custom_call_target="tpu_custom_call" | custom-call | tf_op jit(solution)/shard_map/pallas_call | solution.py:235
  32.8 1.1 %slice_bitcast_fusion.3 = (bf16[2,240,128]{2,1,0:T(8,128)(2,1)S(1)}, bf16[2,240,128]{2,1,0:T(8,128)(2,1)S(1)}, bf16[2,240,128]{2,1,0:T(8,128)(2,1)S(1)}, bf16[2,240,128]{2,1,0:T(8,128)(2,1)S(1)}) fusion(bf16[4,2,240,128]{3,2,1,0:T(8,128)(2,1)} %shard_map.55), kind=kLoop, calls=%fused_computation.4 | loop fusion | bytes 983040 | tf_op jit(solution)/shard_map/convert_element_type | solution.py:265
  33.9 1.0 %maximum_convert_fusion = f32[2,240,512]{2,1,0:T(8,128)} fusion(bf16[2,240,128]{2,1,0:T(8,128)(2,1)S(1)} %get-tuple-element.6, bf16[2,240,128]{2,1,0:T(8,128)(2,1)S(1)} %get-tuple-element.7, bf16[2,240,128]{2,1,0:T(8,128)(2,1)S(1)} %get-tuple-element.8, bf16[2,240,128]{2,1,0:T(8,128)(2,1)S(1)} %get-tuple-element.5), kind=kLoop, calls=%fused_computation | loop fusion | flops 1966080 | bytes 1474560 | tf_op jit(solution)/shard_map/concatenate | solution.py:265

commit v4 on v3

--- a/solution.py
+++ b/solution.py
@@ -170,9 +170,10 @@
             piece = pieces[step]
             z_copies[piece].wait_recv()
             cross[piece].start()
-            near[piece].start()
         if lag <= step < len(pieces) + lag:
             piece = pieces[step - lag]
+            if piece[0]:
+                near[piece].start()
             cross[piece].wait_recv()
             onward[piece].start()
         if step >= 2 * lag:
@@ -190,27 +191,32 @@
                 to = pl.ds(i * VBLK, VBLK)
                 amp[at, to] = (block.T * w_dir[at, to] - block * w_exc[at, to]).astype(jnp.bfloat16)
 
-    def density(k):
-        total = jnp.dot(wide(0, k), amp[pl.ds(0, width)], preferred_element_type=jnp.float32)
+    def density(k, rows):
+        def part(r):
+            return jnp.concatenate([gath[r, k, i, rows] for i in range(own)], axis=1)
+
+        total = jnp.dot(part(0), amp[pl.ds(0, width)], preferred_element_type=jnp.float32)
         for r in range(1, OCC):
-            total += jnp.dot(wide(r, k), amp[pl.ds(r * width, width)], preferred_element_type=jnp.float32)
-        return total
-
+            total += jnp.dot(part(r), amp[pl.ds(r * width, width)], preferred_element_type=jnp.float32)
+        for i in range(own):
+            outgoing[k, i, rows] = total[:, i * VBLK : (i + 1) * VBLK].astype(jnp.bfloat16)
+
+    depth = b_ref.shape[1]
+    half = depth // 32 * 16
     back = {}
     for k in far_first:
-        total = density(k)
-        for i in range(own):
-            outgoing[k, i] = total[:, i * VBLK : (i + 1) * VBLK].astype(jnp.bfloat16)
-        back[k] = remote(outgoing.at[k], out_ref.at[z], r_send.at[k], r_recv.at[k], aux=zs[k])
-        back[k].start()
-    total = density(0)
-    for i in range(own):
-        outgoing[0, i] = total[:, i * VBLK : (i + 1) * VBLK].astype(jnp.bfloat16)
+        for c, rows in enumerate((pl.ds(0, half), pl.ds(half, depth - half))):
+            density(k, rows)
+            back[k, c] = remote(
+                outgoing.at[k, :, rows], out_ref.at[z, :, rows], r_send.at[k, c], r_recv.at[k, c], aux=zs[k]
+            )
+            back[k, c].start()
+    density(0, pl.ds(0, depth))
     store = pltpu.make_async_copy(outgoing.at[0], out_ref.at[z], store_sem)
     store.start()
 
-    for k in far_first[::-1]:
-        back[k].wait_recv()
+    for copy in back.values():
+        copy.wait_recv()
 
     for piece in pieces:
         near[piece].wait_send()
@@ -218,8 +224,8 @@
         onward[piece].wait_send()
         if piece[0]:
             z_copies[piece].wait_send()
-    for k in far_first:
-        back[k].wait_send()
+    for copy in back.values():
+        copy.wait_send()
     store.wait()
 
 
@@ -254,8 +260,8 @@
             dma((n, own)),
             dma((3, n, own)),
             dma((3, n, own)),
-            dma((n,)),
-            dma((n,)),
+            dma((n, 2)),
+            dma((n, 2)),
             dma,
         ],
         compiler_params=pltpu.CompilerParams(

time: 35.6 us -> 35.6 us (level)
  no operation moved by 1% of the time
where the time goes in v4:
time: 35.6 us; the launch traced here: 34.9 us
  Pallas kernels  32.8 us (92%)
  local copies, waits for them, and re-layouts  1.11 us (3%)
  other arithmetic  1.02 us (3%)
    pallas_call x1, Pallas kernels, shards(): pl.pallas_call(functools.partial(kernel, n), out_shape=jax.ShapeDtypeStru...  32.8 us
    convert_element_type x1, local copies, waits for them, and re-layouts, shards(): slots[k].astype(jnp.float32)  1.11 us
    concatenate x1, other arithmetic, shards(): jnp.concatenate([slots[k].astype(jnp.float32) for k in range(n)], axis=2)  1.02 us

profile of v4, /device:TPU:0, one launch (start us, length us, event | category | flops | bytes accessed | tf_op | source)
XLA Modules:
  0.0 34.9 jit_solution(4315133637125263727)
XLA Ops:
  0.0 32.8 %shard_map.55 = bf16[4,2,240,128]{3,2,1,0:T(8,128)(2,1)} custom-call(bf16[2,240,512]{2,1,0:T(8,128)(2,1)} %b_ref.1, s32[8,8]{1,0:T(8,128)} %tile_hbm.1, s32[8]{0:T(128)} %batch_hbm.1, f32[500]{0:T(512)} %occ_hbm.1, f32[1,128]{1,0:T(1,128)} %bitcast.9), custom_call_target="tpu_custom_call" | custom-call | tf_op jit(solution)/shard_map/pallas_call | solution.py:241
  32.8 1.1 %slice_bitcast_fusion.3 = (bf16[2,240,128]{2,1,0:T(8,128)(2,1)S(1)}, bf16[2,240,128]{2,1,0:T(8,128)(2,1)S(1)}, bf16[2,240,128]{2,1,0:T(8,128)(2,1)S(1)}, bf16[2,240,128]{2,1,0:T(8,128)(2,1)S(1)}) fusion(bf16[4,2,240,128]{3,2,1,0:T(8,128)(2,1)} %shard_map.55), kind=kLoop, calls=%fused_computation.4 | loop fusion | bytes 983040 | tf_op jit(solution)/shard_map/convert_element_type | solution.py:271
  33.9 1.0 %maximum_convert_fusion = f32[2,240,512]{2,1,0:T(8,128)} fusion(bf16[2,240,128]{2,1,0:T(8,128)(2,1)S(1)} %get-tuple-element.6, bf16[2,240,128]{2,1,0:T(8,128)(2,1)S(1)} %get-tuple-element.7, bf16[2,240,128]{2,1,0:T(8,128)(2,1)S(1)} %get-tuple-element.8, bf16[2,240,128]{2,1,0:T(8,128)(2,1)S(1)} %get-tuple-element.5), kind=kLoop, calls=%fused_computation | loop fusion | flops 1966080 | bytes 1474560 | tf_op jit(solution)/shard_map/concatenate | solution.py:271
